TPU v7x, 32 devices: a whole 2x2x4 slice. The times are simulated.
32 devices in a mesh: gx: 4 (over z), gy: 4 (over y, x), gz: 2 (over core).
Axes of the slice: x: 2, y: 2, z: 4, core: 2. Of those that a mesh axis runs over, the one named last changes fastest.
Arguments:
- links: bfloat16 [4, 4, 16, 2, 9, 64, 128], P('gx', 'gy', 'gz'), may hold values from -0.5 to 0.5
- null_vectors: bfloat16 [4, 4, 16, 2, 32, 128], P('gx', 'gy', 'gz'), may hold values from -1.796875 to 1.796875
- offsets: int32 [9, 4], replicated, may hold values from -1 to 1, as said below
- place: int32 [2, 2, 8, 1], replicated, may hold values from 0 to 7, as said below
Outputs:
- coarse_links: float32 [4, 2, 4, 9, 2048], P('gx', 'gz')
Inputs may be any that keep to these rules, and one draw needn't show every extreme that they name: The rows are the nine offsets zero, plus one and minus one along each of x, y, z, t, each once, in some order. `place`: for each cx and each aligned run of 4 values of cz, the values over all cy, those cz and all ct are each of 0 to 7 once.
All inputs are finite; a program needn't handle non-finite values.
Results may differ from a plain program's by a relative error of at most 0.0029.
Values may be sent and summed in bfloat16 or wider, within the bound.
A program may use at most 64 MiB of HBM per device.

v0:
```python
import jax
import jax.numpy as jnp
from jax import lax
from jax.sharding import PartitionSpec as P

STANDARD = (
    (0, 0, 0, 0),
    (1, 0, 0, 0),
    (-1, 0, 0, 0),
    (0, 1, 0, 0),
    (0, -1, 0, 0),
    (0, 0, 1, 0),
    (0, 0, -1, 0),
    (0, 0, 0, 1),
    (0, 0, 0, -1),
)


def with_halo(block, sides, width):
    for axis, dim in sides:
        count = lax.axis_size(axis)
        forward = [(i, i + 1) for i in range(count - 1)]
        forward.append((count - 1, 0))
        backward = [(target, source) for source, target in forward]
        low = lax.ppermute(
            lax.slice_in_dim(block, block.shape[dim] - width, None, axis=dim), axis, forward
        )
        high = lax.ppermute(lax.slice_in_dim(block, 0, width, axis=dim), axis, backward)
        block = jnp.concatenate([low, block, high], axis=dim)
    return block


def partner(value, axis, distance):
    mask = 2**distance
    pairs = [(source, source ^ mask) for source in range(lax.axis_size(axis))]
    return lax.ppermute(value, axis, pairs)


def neighbour_blocks(neighbour):
    half_width = neighbour.shape[-1] // 2
    real_part = neighbour[..., :half_width]
    imag_part = neighbour[..., half_width:]
    upper_rows = jnp.concatenate([real_part, -imag_part], -1)
    lower_rows = jnp.concatenate([imag_part, real_part], -1)
    return jnp.concatenate([upper_rows, lower_rows], -2)


def conj_blocks(hopped):
    half_width = hopped.shape[-1] // 2
    hop_real = hopped[..., :half_width]
    hop_imag = hopped[..., half_width:]
    return jnp.concatenate([hopped, jnp.concatenate([hop_imag, -hop_real], -1)], -2)


def local(links, null_vectors, offsets, place):
    z_len = links.shape[2]
    t_len = links.shape[3]
    vec_count = null_vectors.shape[4]
    flat_width = 2 * vec_count * vec_count
    widened = with_halo(null_vectors, (("gx", 0), ("gy", 1), ("gz", 2)), 1)
    candidates = []
    for offset_row in STANDARD:
        shard_piece = widened[
            1 + offset_row[0], 1 + offset_row[1], 1 + offset_row[2] : 1 + offset_row[2] + z_len
        ]
        candidates.append(jnp.roll(shard_piece, -offset_row[3], axis=1))
    stacked = jnp.stack(candidates)
    standard_table = jnp.array(STANDARD, jnp.int32)
    matched = jnp.all(offsets[:, None, :] == standard_table[None, :, :], axis=-1).astype(jnp.int32)
    chosen = jnp.sum(matched * jnp.arange(9, dtype=jnp.int32)[None, :], axis=1)
    neighbour = jnp.take(stacked, chosen, axis=0)
    local_links = links[0, 0]
    hopped = jnp.einsum(
        "ztkrc,kztuc->ztkru",
        local_links,
        neighbour_blocks(neighbour),
        preferred_element_type=jnp.float32,
    ).astype(jnp.bfloat16)
    own_vectors = null_vectors[0, 0]
    coarse = jnp.einsum(
        "ztvq,ztkqu->ztkvu", own_vectors, conj_blocks(hopped), preferred_element_type=jnp.float32
    )
    x_sign = lax.axis_index("gx") % 2 * 2 - 1
    y_sign = lax.axis_index("gy") % 2 * 2 - 1
    z_sign = jnp.arange(z_len, dtype=jnp.int32) % 2 * 2 - 1
    t_sign = jnp.arange(t_len, dtype=jnp.int32) % 2 * 2 - 1
    outside = (
        (offsets[:, 0] == x_sign).astype(jnp.float32)[None, None, :]
        + (offsets[:, 1] == y_sign).astype(jnp.float32)[None, None, :]
        + (offsets[None, :, 2] == z_sign[:, None]).astype(jnp.float32)[:, None, :]
        + (offsets[None, :, 3] == t_sign[:, None]).astype(jnp.float32)[None, :, :]
    )
    is_self = jnp.all(offsets == 0, axis=1).astype(jnp.float32)
    spilled = jnp.sum((1.0 - outside)[..., None, None] * coarse, axis=2)
    contrib = (
        outside[..., None, None] * coarse + is_self[None, None, :, None, None] * spilled[:, :, None]
    )
    q_count = z_len // 2 * (t_len // 2)
    partial_value = contrib.reshape(z_len // 2, 2, t_len // 2, 2, 9, flat_width).sum(axis=(1, 3))
    partial_value = partial_value.reshape(q_count, 9, flat_width)
    partial_value = partial_value + partner(partial_value, "gx", 0)
    partial_value = partial_value + partner(partial_value, "gy", 0)
    y_half = lax.axis_index("gy") % 2
    sendable = lax.dynamic_slice_in_dim(partial_value, y_half * (q_count // 2), q_count // 2, 0)
    column_count = place.shape[1]
    my_column = lax.axis_index("gx") % 2
    line_places = lax.dynamic_slice(
        place,
        (lax.axis_index("gx") // 2, 0, lax.axis_index("gz") * (z_len // 2), 0),
        (1, column_count, z_len // 2, t_len // 2),
    )
    line_places = line_places.reshape(column_count, q_count)
    capacity = column_count * q_count // 2
    incoming = lax.all_gather(sendable[None], "gy", axis=0, tiled=True)
    row_count = incoming.shape[0]
    sender = jnp.arange(row_count, dtype=jnp.int32)
    positions = jnp.take(line_places, sender // 2, axis=0)
    picked = (sender % 2)[:, None] * (q_count // 2) + jnp.arange(q_count // 2, dtype=jnp.int32)[
        None, :
    ]
    positions = jnp.take_along_axis(positions, picked, axis=1)
    is_mine = positions // capacity == my_column
    slot_index = positions % capacity
    onehot = (
        (slot_index[..., None] == jnp.arange(capacity, dtype=jnp.int32)) & is_mine[..., None]
    ).astype(jnp.float32)
    gathered = jnp.einsum("nqs,nqkf->skf", onehot, incoming, precision=lax.Precision.HIGHEST)
    return gathered[None, None]


def solution(mesh):
    placed = (
        P("gx", "gy", "gz", None, None, None, None),
        P("gx", "gy", "gz", None, None, None),
        P(),
        P(),
    )
    return jax.shard_map(
        local,
        mesh=mesh,
        in_specs=placed,
        out_specs=P("gx", "gz", None, None, None),
        check_vma=False,
    )
```

profile of v0, /device:TPU:0, one launch (start us, length us, event | category | flops | bytes accessed | tf_op | source)
XLA Modules:
  0.0 92.5 jit_solution(16244818165478859596)
XLA Ops:
  0.0 3.0 %collective-permute-start.1 = (bf16[1,1,8,2,32,128]{5,4,3,2,1,0:T(8,128)(2,1)}, bf16[1,1,8,2,32,128]{5,4,3,2,1,0:T(8,128)(2,1)}, u32[]{:S(2)}, u32[]{:S(2)}) collective-permute-start(bf16[1,1,8,2,32,128]{5,4,3,2,1,0:T(8,128)(2,1)} %param.6), channel_id=1, source_target_pairs={{0,8},{8,16},{16,24},{24,0},{1,9},{9,17},{17,25},{25,1},{2,10},{10... | collective-permute-start | bytes 393224 | tf_op jit(solution)/shard_map/ppermute | solution.py:25
  3.0 2.1 %collective-permute-start = (bf16[1,1,8,2,32,128]{5,4,3,2,1,0:T(8,128)(2,1)}, bf16[1,1,8,2,32,128]{5,4,3,2,1,0:T(8,128)(2,1)}, u32[]{:S(2)}, u32[]{:S(2)}) collective-permute-start(bf16[1,1,8,2,32,128]{5,4,3,2,1,0:T(8,128)(2,1)} %param.6), channel_id=1, source_target_pairs={{8,0},{16,8},{24,16},{0,24},{9,1},{17,9},{25,17},{1,25},{10,2},{18... | collective-permute-start | bytes 393224 | tf_op jit(solution)/shard_map/ppermute | solution.py:28
  5.1 0.5 fusion.51
  5.7 0.6 fusion.49
  6.3 0.6 fusion.44
  6.8 0.7 compare_reduce_fusion.1
  7.5 1.3 %slice_bitcast_fusion.3 = (s32[9]{0:T(128)}, s32[9]{0:T(128)}) fusion(s32[9,4]{0,1:T(4,128)} %param.7), kind=kLoop, calls=%fused_computation.116 | loop fusion | bytes 144 | tf_op jit(solution)/shard_map/eq | solution.py:90
  8.9 0.8 copy.31
  9.7 0.9 bitcast_dynamic-update-slice_fusion.2
  10.6 0.6 convert_element_type.51
  11.2 0.1 fusion.36
  11.2 0.1 reshape.358
  11.3 0.8 compare_reduce_fusion
  12.1 0.1 select_reduce_fusion
  12.2 0.5 copy-done.10
  12.7 1.5 %fusion.57 = (bf16[8,1,32,128]{3,2,1,0:T(8,128)(2,1)}, bf16[8,1,32,128]{3,2,1,0:T(8,128)(2,1)}) fusion(bf16[8,2,32,128]{3,2,1,0:T(8,128)(2,1)} %bitcast.76), kind=kLoop, calls=%fused_computation.122 | loop fusion | bytes 262144 | tf_op jit(solution)/shard_map/jit(_roll_static)/slice | solution.py:66
  14.3 0.8 fusion.47
  15.0 1.2 %compare_convert_fusion = f32[2,9]{1,0:T(2,128)} fusion(s32[9]{0:T(128)} %get-tuple-element.19, s32[2]{0:T(128)} %fusion.51), kind=kLoop, calls=%fused_computation.88 | loop fusion | flops 36 | bytes 116 | tf_op jit(solution)/shard_map/convert_element_type | solution.py:91
  16.3 1.3 %pad_clamp_fusion = (s32[1024]{0:T(1024)}, s32[1024]{0:T(1024)S(1)}) fusion(s32[9]{0:T(128)S(1)} %fusion.52, s32[4]{0:T(128)} %fusion.44), kind=kLoop, calls=%fused_computation.58 | loop fusion | flops 2048 | bytes 8244 | tf_op jit(solution)/shard_map/jit(_take)/gather | solution.py:71
  17.5 0.8 constant_dynamic-slice_fusion
  18.3 1.1 %gather_fusion = s32[4,4]{1,0:T(4,128)} fusion(s32[2,4]{1,0:T(2,128)S(1)} %bitcast.77, s32[1024]{0:T(1024)S(1)} %get-tuple-element.23), kind=kCustom, calls=%fused_computation | custom fusion | bytes 144 | tf_op jit(solution)/shard_map/jit(_take)/gather | solution.py:117
  19.4 0.8 convert_add_fusion
  20.2 1.2 %broadcast_add_fusion = (f32[8,2,9]{2,1,0:T(2,128)S(1)}, f32[8,2,9]{2,1,0:T(2,128)}) fusion(f32[2,9]{1,0:T(2,128)} %compare_convert_fusion, f32[8,9]{1,0:T(8,128)S(1)} %convert_add_fusion), kind=kLoop, calls=%fused_computation.61 | loop fusion | flops 288 | bytes 1512 | tf_op jit(solution)/shard_map/add | solution.py:88
  21.4 0.6 compare_and_fusion
  22.0 0.9 constant_dynamic-update-slice_fusion.2
  22.9 0.9 constant_dynamic-update-slice_fusion.1
  23.9 0.9 constant_dynamic-update-slice_fusion
  24.8 1.7 %collective-permute-start.3 = (bf16[3,1,8,2,32,128]{5,4,3,2,1,0:T(8,128)(2,1)S(1)}, bf16[3,1,8,2,32,128]{5,4,3,2,1,0:T(8,128)(2,1)S(1)}, u32[]{:S(2)}, u32[]{:S(2)}) collective-permute-start(bf16[3,1,8,2,32,128]{5,4,3,2,1,0:T(8,128)(2,1)S(1)} %constant_dynamic-update-slice_fusion), channel_id=1, source_target_pairs={{0,2},{2,4},{4,6},{6,0},{1,3},{3,5},{5,7},{7,1},{8,10},{10,12},{12... | collective-permute-start | bytes 1179656 | tf_op jit(solution)/shard_map/ppermute | solution.py:25
  26.5 1.3 %collective-permute-start.2 = (bf16[3,1,8,2,32,128]{5,4,3,2,1,0:T(8,128)(2,1)S(1)}, bf16[3,1,8,2,32,128]{5,4,3,2,1,0:T(8,128)(2,1)S(1)}, u32[]{:S(2)}, u32[]{:S(2)}) collective-permute-start(bf16[3,1,8,2,32,128]{5,4,3,2,1,0:T(8,128)(2,1)S(1)} %constant_dynamic-update-slice_fusion), channel_id=1, source_target_pairs={{2,0},{4,2},{6,4},{0,6},{3,1},{5,3},{7,5},{1,7},{10,8},{12,10},{14... | collective-permute-start | bytes 1179656 | tf_op jit(solution)/shard_map/ppermute | solution.py:28
  27.8 0.9 bitcast_dynamic-update-slice_fusion.1
  28.7 0.9 bitcast_dynamic-update-slice_fusion
  29.6 8.2 %collective-permute-done.3 = bf16[3,1,8,2,32,128]{5,4,3,2,1,0:T(8,128)(2,1)S(1)} collective-permute-done((bf16[3,1,8,2,32,128]{5,4,3,2,1,0:T(8,128)(2,1)S(1)}, bf16[3,1,8,2,32,128]{5,4,3,2,1,0:T(8,128)(2,1)S(1)}, u32[]{:S(2)}, u32[]{:S(2)}) %collective-permute-start.3) | collective-permute-done | bytes 393248 | tf_op jit(solution)/shard_map/ppermute | solution.py:25
  37.8 7.0 %collective-permute-done.2 = bf16[3,1,8,2,32,128]{5,4,3,2,1,0:T(8,128)(2,1)S(1)} collective-permute-done((bf16[3,1,8,2,32,128]{5,4,3,2,1,0:T(8,128)(2,1)S(1)}, bf16[3,1,8,2,32,128]{5,4,3,2,1,0:T(8,128)(2,1)S(1)}, u32[]{:S(2)}, u32[]{:S(2)}) %collective-permute-start.2) | collective-permute-done | bytes 393248 | tf_op jit(solution)/shard_map/ppermute | solution.py:28
  44.9 0.1 collective-permute-start.5
  44.9 0.5 collective-permute-start.4
  45.5 0.0 copy-start.3
  45.5 1.0 %collective-permute-done.4 = bf16[3,3,1,2,32,128]{5,4,3,2,1,0:T(8,128)(2,1)S(1)} collective-permute-done((bf16[3,3,1,2,32,128]{5,4,3,2,1,0:T(8,128)(2,1)S(1)}, bf16[3,3,1,2,32,128]{5,4,3,2,1,0:T(8,128)(2,1)S(1)}, u32[]{:S(2)}, u32[]{:S(2)}) %collective-permute-start.4) | collective-permute-done | bytes 147488 | tf_op jit(solution)/shard_map/ppermute | solution.py:28
  46.6 1.0 %copy-done.1 = bf16[9,8,2,32,128]{4,3,2,1,0:T(8,128)(2,1)} copy-done((bf16[9,8,2,32,128]{4,3,2,1,0:T(8,128)(2,1)}, bf16[9,8,2,32,128]{4,3,2,1,0:T(8,128)(2,1)S(1)}, u32[]{:S(2)}) %copy-start.1) | copy-done | bytes 1179672
  47.7 2.2 %gather_fusion.1 = bf16[9,8,2,32,128]{4,3,2,1,0:T(8,128)(2,1)S(1)} fusion(bf16[9,8,2,32,128]{4,3,2,1,0:T(8,128)(2,1)} %copy-done.1, s32[1024]{0:T(1024)} %get-tuple-element.22), kind=kCustom, calls=%fused_computation.1 | custom fusion | bytes 2359332 | tf_op jit(solution)/shard_map/jit(_take)/gather | solution.py:71
  49.8 0.2 copy_select_fusion
  50.0 0.5 slice_negate_fusion.1
  50.5 1.8 %convert_bitcast_fusion = bf16[8,2,9,64,64]{3,4,2,1,0:T(8,128)(2,1)S(1)} fusion(bf16[1,1,8,2,9,64,128]{6,5,4,3,2,1,0:T(8,128)(2,1)S(1)} %copy-done, bf16[9,8,2,32,64]{4,3,0,2,1:T(8,128)(2,1)S(1)} %get-tuple-element.11, bf16[9,8,2,32,64]{4,3,0,2,1:T(8,128)(2,1)S(1)} %get-tuple-element.10, bf16[9,8,2,32,64]{4,3,0,2,1:T(8,128)(2,1)S(1)} %get-tuple-element.9), kind=kOutput, calls=%fused_computation.21 | convolution fusion | flops 161021952 | bytes 5308416 | tf_op jit(solution)/shard_map/ztkrc,kztuc->ztkru/dot_general | solution.py:73
  52.4 0.2 fusion.56
  52.6 0.6 copy-done.2
  53.3 2.6 %multiply_reduce_fusion = (f32[8,2,64,32]{2,3,1,0:T(8,128)S(1)}, f32[8,2,9,64,32]{3,4,2,1,0:T(8,128)S(1)}) fusion(f32[8,2,9]{2,1,0:T(2,128)S(1)} %copy-done.6, bf16[1,1,8,2,32,128]{5,4,3,2,1,0:T(8,128)(2,1)S(1)} %copy-done.2, bf16[8,2,9,64,32]{3,4,2,1,0:T(8,128)(2,1)S(1)} %get-tuple-element.8, bf16[8,2,9,64,32]{3,4,2,1,0:T(8,128)(2,1)S(1)} %get-tuple-element.7, ...), kind=kOutput, calls=%fused_computation.20 | convolution fusion | flops 83132416 | bytes 3801664 | tf_op jit(solution)/shard_map/ztvq,ztkqu->ztkvu/dot_general | solution.py:80
  55.8 0.5 fusion.14
  56.3 1.4 %reshape.368 = f32[4,2,9,2048]{3,2,1,0:T(8,128)} reshape(f32[8,9,32,64]{3,2,1,0:T(8,128)S(1)} %fusion.14) | data formatting | bytes 1179648 | tf_op jit(solution)/shard_map/reduce_sum | solution.py:99
  57.7 1.3 %reduce_sum.44 = f32[4,9,2048]{2,1,0:T(8,128)S(1)} reduce(f32[4,2,9,2048]{3,2,1,0:T(8,128)} %reshape.368, f32[]{:T(128)} %constant.168.clone.1), dimensions={1}, to_apply=%region_5.6 | reduce | flops 73728 | bytes 884740 | tf_op jit(solution)/shard_map/reduce_sum | solution.py:99
  59.1 0.2 copy.42
  59.3 0.1 collective-permute-start.6
  59.4 0.1 broadcast_select_fusion
  59.4 0.7 gather_fusion.2
  60.1 0.1 reshape.361
  60.2 8.4 %collective-permute-done.6 = f32[4,9,2048]{2,0,1:T(4,128)S(1)} collective-permute-done((f32[4,9,2048]{2,0,1:T(4,128)S(1)}, f32[4,9,2048]{2,0,1:T(4,128)S(1)}, u32[]{:S(2)}, u32[]{:S(2)}) %collective-permute-start.6) | collective-permute-done | bytes 294944 | tf_op jit(solution)/shard_map/ppermute | solution.py:36
  68.5 0.2 copy_add_fusion
  68.8 1.6 %collective-permute-start.7 = (f32[4,9,2048]{2,0,1:T(4,128)S(1)}, f32[4,9,2048]{2,0,1:T(4,128)S(1)}, u32[]{:S(2)}, u32[]{:S(2)}) collective-permute-start(f32[4,9,2048]{2,0,1:T(4,128)S(1)} %copy_add_fusion), channel_id=1, source_target_pairs={{0,2},{2,0},{4,6},{6,4},{1,3},{3,1},{5,7},{7,5},{8,10},{10,8},{12,... | collective-permute-start | bytes 884744 | tf_op jit(solution)/shard_map/ppermute | solution.py:36
  70.3 0.1 fusion.33
  70.4 0.1 copy.30
  70.5 0.1 copy.29
  70.6 6.6 %collective-permute-done.7 = f32[4,9,2048]{2,0,1:T(4,128)S(1)} collective-permute-done((f32[4,9,2048]{2,0,1:T(4,128)S(1)}, f32[4,9,2048]{2,0,1:T(4,128)S(1)}, u32[]{:S(2)}, u32[]{:S(2)}) %collective-permute-start.7) | collective-permute-done | bytes 294944 | tf_op jit(solution)/shard_map/ppermute | solution.py:36
  77.2 0.1 dynamic-slice_add_fusion
  77.4 0.1 copy.34
  77.5 13.3 %all-gather = f32[8,9,2048]{2,1,0:T(8,128)S(1)} all-gather(f32[2,9,2048]{2,1,0:T(8,128)S(1)} %copy.34), channel_id=2, replica_groups=mesh['gx'=4,'gy'=4,'gz'=2] {'gy'}, dimensions={0}, use_global_device_ids=true | all-gather | bytes 737280 | tf_op jit(solution)/shard_map/all_gather | solution.py:114
  90.8 1.7 %convolution_bitcast_fusion = f32[1,1,4,9,2048]{4,2,3,1,0:T(4,128)} fusion(f32[4,2,9,2048]{3,2,1,0:T(8,128)S(1)} %bitcast.75, s32[4,2]{0,1:T(2,128)S(1)} %copy.29, pred[4,2]{0,1:T(4,128)(4,1)S(1)} %copy.30), kind=kOutput, calls=%fused_computation.22 | convolution fusion | flops 7077952 | bytes 884776 | tf_op jit(solution)/shard_map/nqs,nqkf->skf/dot_general | solution.py:127
  (32 shorter events, 0.2 us)
Async XLA Ops:
  0.0 50.5 %copy-start = (bf16[1,1,8,2,9,64,128]{6,5,4,3,2,1,0:T(8,128)(2,1)S(1)}, bf16[1,1,8,2,9,64,128]{6,5,4,3,2,1,0:T(8,128)(2,1)}, u32[]{:S(2)}) copy-start(bf16[1,1,8,2,9,64,128]{6,5,4,3,2,1,0:T(8,128)(2,1)} %param.5) | copy-start | bytes 7077892
  0.0 22.0 %collective-permute-start.1 = (bf16[1,1,8,2,32,128]{5,4,3,2,1,0:T(8,128)(2,1)}, bf16[1,1,8,2,32,128]{5,4,3,2,1,0:T(8,128)(2,1)}, u32[]{:S(2)}, u32[]{:S(2)}) collective-permute-start(bf16[1,1,8,2,32,128]{5,4,3,2,1,0:T(8,128)(2,1)} %param.6), channel_id=1, source_target_pairs={{0,8},{8,16},{16,24},{24,0},{1,9},{9,17},{17,25},{25,1},{2,10},{10... | collective-permute-start | bytes 393224 | tf_op jit(solution)/shard_map/ppermute | solution.py:25
  3.0 20.8 %collective-permute-start = (bf16[1,1,8,2,32,128]{5,4,3,2,1,0:T(8,128)(2,1)}, bf16[1,1,8,2,32,128]{5,4,3,2,1,0:T(8,128)(2,1)}, u32[]{:S(2)}, u32[]{:S(2)}) collective-permute-start(bf16[1,1,8,2,32,128]{5,4,3,2,1,0:T(8,128)(2,1)} %param.6), channel_id=1, source_target_pairs={{8,0},{16,8},{24,16},{0,24},{9,1},{17,9},{25,17},{1,25},{10,2},{18... | collective-permute-start | bytes 393224 | tf_op jit(solution)/shard_map/ppermute | solution.py:28
  5.1 6.1 %copy-start.7 = (s32[4]{0:T(128)}, s32[4]{0:T(128)S(1)}, u32[]{:S(2)}) copy-start(s32[4]{0:T(128)S(1)} %fusion.45) | copy-start | bytes 52
  12.2 0.5 copy-start.10
  24.8 13.0 %collective-permute-start.3 = (bf16[3,1,8,2,32,128]{5,4,3,2,1,0:T(8,128)(2,1)S(1)}, bf16[3,1,8,2,32,128]{5,4,3,2,1,0:T(8,128)(2,1)S(1)}, u32[]{:S(2)}, u32[]{:S(2)}) collective-permute-start(bf16[3,1,8,2,32,128]{5,4,3,2,1,0:T(8,128)(2,1)S(1)} %constant_dynamic-update-slice_fusion), channel_id=1, source_target_pairs={{0,2},{2,4},{4,6},{6,0},{1,3},{3,5},{5,7},{7,1},{8,10},{10,12},{12... | collective-permute-start | bytes 1179656 | tf_op jit(solution)/shard_map/ppermute | solution.py:25
  26.5 18.3 %collective-permute-start.2 = (bf16[3,1,8,2,32,128]{5,4,3,2,1,0:T(8,128)(2,1)S(1)}, bf16[3,1,8,2,32,128]{5,4,3,2,1,0:T(8,128)(2,1)S(1)}, u32[]{:S(2)}, u32[]{:S(2)}) collective-permute-start(bf16[3,1,8,2,32,128]{5,4,3,2,1,0:T(8,128)(2,1)S(1)} %constant_dynamic-update-slice_fusion), channel_id=1, source_target_pairs={{2,0},{4,2},{6,4},{0,6},{3,1},{5,3},{7,5},{1,7},{10,8},{12,10},{14... | collective-permute-start | bytes 1179656 | tf_op jit(solution)/shard_map/ppermute | solution.py:28
  44.9 1.7 %collective-permute-start.5 = (bf16[3,3,1,2,32,128]{5,4,3,2,1,0:T(8,128)(2,1)S(1)}, bf16[3,3,1,2,32,128]{5,4,3,2,1,0:T(8,128)(2,1)S(1)}, u32[]{:S(2)}, u32[]{:S(2)}) collective-permute-start(bf16[3,3,1,2,32,128]{5,4,3,2,1,0:T(8,128)(2,1)S(1)} %get-tuple-element.12), channel_id=1, source_target_pairs={{0,1},{1,0},{2,3},{3,2},{4,5},{5,4},{6,7},{7,6},{8,9},{9,8},{10,11... | collective-permute-start | bytes 442376 | tf_op jit(solution)/shard_map/ppermute | solution.py:25
  44.9 1.6 %collective-permute-start.4 = (bf16[3,3,1,2,32,128]{5,4,3,2,1,0:T(8,128)(2,1)S(1)}, bf16[3,3,1,2,32,128]{5,4,3,2,1,0:T(8,128)(2,1)S(1)}, u32[]{:S(2)}, u32[]{:S(2)}) collective-permute-start(bf16[3,3,1,2,32,128]{5,4,3,2,1,0:T(8,128)(2,1)S(1)} %get-tuple-element.13), channel_id=1, source_target_pairs={{1,0},{0,1},{3,2},{2,3},{5,4},{4,5},{7,6},{6,7},{9,8},{8,9},{11,10... | collective-permute-start | bytes 442376 | tf_op jit(solution)/shard_map/ppermute | solution.py:28
  45.5 1.1 %copy-start.3 = (bf16[8,1,32,128]{3,2,1,0:T(8,128)(2,1)S(1)}, bf16[8,1,32,128]{3,2,1,0:T(8,128)(2,1)}, u32[]{:S(2)}) copy-start(bf16[8,1,32,128]{3,2,1,0:T(8,128)(2,1)} %get-tuple-element.14) | copy-start | bytes 196612
  45.5 1.1 %copy-start.4 = (bf16[8,1,32,128]{3,2,1,0:T(8,128)(2,1)S(1)}, bf16[8,1,32,128]{3,2,1,0:T(8,128)(2,1)}, u32[]{:S(2)}) copy-start(bf16[8,1,32,128]{3,2,1,0:T(8,128)(2,1)} %get-tuple-element.15) | copy-start | bytes 196612
  46.6 1.0 %copy-start.1 = (bf16[9,8,2,32,128]{4,3,2,1,0:T(8,128)(2,1)}, bf16[9,8,2,32,128]{4,3,2,1,0:T(8,128)(2,1)S(1)}, u32[]{:S(2)}) copy-start(bf16[9,8,2,32,128]{4,3,2,1,0:T(8,128)(2,1)S(1)} %fusion.29) | copy-start | bytes 3538948
  52.3 0.9 copy-start.2
  52.4 0.9 copy-start.6
  53.3 2.6 %copy-start.9 = (f32[9]{0:T(128)S(1)}, f32[9]{0:T(128)}, u32[]{:S(2)}) copy-start(f32[9]{0:T(128)} %convert_element_type.51) | copy-start | bytes 112
  57.7 1.6 %copy-start.5 = (s32[4,4]{1,0:T(4,128)S(1)}, s32[4,4]{1,0:T(4,128)}, u32[]{:S(2)}) copy-start(s32[4,4]{1,0:T(4,128)} %gather_fusion) | copy-start | bytes 196
  59.3 9.3 %collective-permute-start.6 = (f32[4,9,2048]{2,0,1:T(4,128)S(1)}, f32[4,9,2048]{2,0,1:T(4,128)S(1)}, u32[]{:S(2)}, u32[]{:S(2)}) collective-permute-start(f32[4,9,2048]{2,0,1:T(4,128)S(1)} %copy.42), channel_id=1, source_target_pairs={{0,8},{8,0},{16,24},{24,16},{1,9},{9,1},{17,25},{25,17},{2,10},{10... | collective-permute-start | bytes 884744 | tf_op jit(solution)/shard_map/ppermute | solution.py:36
  59.4 10.9 %copy-start.8 = (s32[4]{0:T(128)S(1)}, s32[4]{0:T(128)}, u32[]{:S(2)}) copy-start(s32[4]{0:T(128)} %copy-done.7) | copy-start | bytes 52
  68.8 8.5 %collective-permute-start.7 = (f32[4,9,2048]{2,0,1:T(4,128)S(1)}, f32[4,9,2048]{2,0,1:T(4,128)S(1)}, u32[]{:S(2)}, u32[]{:S(2)}) collective-permute-start(f32[4,9,2048]{2,0,1:T(4,128)S(1)} %copy_add_fusion), channel_id=1, source_target_pairs={{0,2},{2,0},{4,6},{6,4},{1,3},{3,1},{5,7},{7,5},{8,10},{10,8},{12,... | collective-permute-start | bytes 884744 | tf_op jit(solution)/shard_map/ppermute | solution.py:36
where the time goes:
time: 93.1 us; the launch traced here: 92.5 us
  waiting for transfers between devices  31.2 us (34%)
  local copies, waits for them, and re-layouts  18.2 us (20%)
  blocking collectives  13.3 us (14%)
  other arithmetic  13.2 us (14%)
  starting transfers between devices  10.3 us (11%)
  matrix products  6.06 us (7%)
    ppermute x2, waiting for transfers between devices, partner(): return lax.ppermute(value, axis, pairs)  15 us
    all_gather x1, blocking collectives, local(): incoming = lax.all_gather(sendable[None], 'gy', axis=0, tiled=True)  13.3 us
    ppermute x3, waiting for transfers between devices, with_halo(): lax.ppermute(lax.slice_in_dim(block, block.shape[dim] - width, None, axis...  8.17 us
    ppermute x3, waiting for transfers between devices, with_halo(): lax.ppermute(lax.slice_in_dim(block, 0, width, axis=dim), axis, backward)  8.02 us
    unnamed x31, local copies, waits for them, and re-layouts  7.8 us
    ppermute x3, starting transfers between devices, with_halo(): lax.ppermute(lax.slice_in_dim(block, block.shape[dim] - width, None, axis...  4.8 us
    ppermute x3, starting transfers between devices, with_halo(): lax.ppermute(lax.slice_in_dim(block, 0, width, axis=dim), axis, backward)  3.85 us
    add x3, other arithmetic, local(): (offsets[:, 0] == x_sign).astype(jnp.float32)[None, None, :]  2.76 us
  transfers between devices with their start and end apart: 8, of which 5 were waited for; matrix products, arithmetic and copies ran while one was open for 23% of the time, Pallas kernels for 0%

commit v1 on v0

v1 whole, which is shorter than its diff:
```python
import functools

import jax
import jax.numpy as jnp
from jax import lax
from jax.experimental import pallas as pl
from jax.experimental.pallas import tpu as pltpu
from jax.sharding import PartitionSpec as P

MESH = pl.DeviceIdType.MESH
F32 = jnp.float32
BF16 = jnp.bfloat16
ZT, ALL, PART = 4, 9, 7


def rotated(value):
    half = value.shape[-1] // 2
    return pltpu.roll(value, half, 1)


def right_blocks(vectors):
    value = vectors.astype(F32)
    half = value.shape[-1] // 2
    lane = lax.broadcasted_iota(jnp.int32, value.shape, 1)
    first = jnp.where(lane < half, value, -value)
    second = rotated(value)
    return jnp.concatenate([first, second, second, -first], 0).astype(BF16)


def hop(left, right):
    return lax.dot_general(
        left, right, (((1,), (1,)), ((), ())), preferred_element_type=F32
    ).astype(BF16)


def mm(left, right):
    return jnp.dot(left, right, preferred_element_type=F32)


def fold(product):
    rows = product.shape[0] // 4
    a, b, c, d = (product[i * rows : (i + 1) * rows] for i in range(4))
    lane = lax.broadcasted_iota(jnp.int32, a.shape, 1)
    return jnp.where(lane < a.shape[1] // 2, a + rotated(c), rotated(b) + d)


def kernel(
    sizes,
    links_hbm,
    vec_hbm,
    offsets_ref,
    place_ref,
    out_ref,
    links,
    vec,
    halo,
    halo_z,
    blocks,
    vec32,
    left,
    left_t,
    acc,
    own,
    sendbuf,
    arrived,
    gathered,
    flat,
    link_sem,
    vec_sem,
    hs_sem,
    hr_sem,
    zs_sem,
    zr_sem,
    rs_sem,
    rr_sem,
    gs_sem,
    gr_sem,
):
    n_gx, n_gy, n_gz = sizes
    z_len, t_len, n_vec = vec.shape[0], vec.shape[1], vec.shape[2]
    n_comp = links.shape[3]
    q_count = z_len // 2
    gx, gy, gz = lax.axis_index("gx"), lax.axis_index("gy"), lax.axis_index("gz")
    xb, yb = gx % 2, gy % 2
    x_out = (gx + 2 * xb - 1 + n_gx) % n_gx
    x_in = gx + 1 - 2 * xb
    y_out = (gy + 2 * yb - 1 + n_gy) % n_gy
    y_in = gy + 1 - 2 * yb
    z_up, z_down = (gz + 1) % n_gz, (gz + n_gz - 1) % n_gz

    peers = []
    for dx in range(2):
        for dy in range(n_gy):
            if dx or dy:
                peers.append((dx, dy, (gx + dx * (1 - 2 * xb), (gy + dy) % n_gy, gz)))

    barrier = pltpu.get_barrier_semaphore()
    for _, _, device in peers:
        pl.semaphore_signal(barrier, inc=1, device_id=device, device_id_type=MESH)
    for device in ((x_out, gy, gz), (gx, gy, z_up), (gx, gy, z_down)):
        pl.semaphore_signal(barrier, inc=1, device_id=device, device_id_type=MESH)

    vec_copy = pltpu.make_async_copy(vec_hbm.at[0, 0], vec, vec_sem)
    vec_copy.start()

    def square(d):
        return (xb + d % 2) % 2 + 2 * ((yb + d // 2) % 2)

    link_copy = pltpu.make_async_copy(links_hbm.at[0, 0], links, link_sem)
    link_copy.start()

    codes = [
        offsets_ref[0, k] + 3 * offsets_ref[1, k] + 9 * offsets_ref[2, k] + 27 * offsets_ref[3, k]
        for k in range(ALL)
    ]

    def position(code):
        found = jnp.int32(0)
        for k in range(1, ALL):
            found = jnp.where(codes[k] == code, k, found)
        return found

    x_sign, y_sign = 2 * xb - 1, 2 * yb - 1
    k_zero = position(0)
    k_zp, k_zm, k_tp, k_tm = position(9), position(-9), position(27), position(-27)
    k_dirs = (position(-x_sign), position(x_sign), position(-3 * y_sign), position(3 * y_sign))

    vec_copy.wait()
    pl.semaphore_wait(barrier, len(peers) + 3)

    up_copy = pltpu.make_async_remote_copy(
        src_ref=vec.at[z_len - 1],
        dst_ref=halo_z.at[0],
        send_sem=zs_sem.at[0],
        recv_sem=zr_sem.at[0],
        device_id=(gx, gy, z_up),
        device_id_type=MESH,
    )
    down_copy = pltpu.make_async_remote_copy(
        src_ref=vec.at[0],
        dst_ref=halo_z.at[1],
        send_sem=zs_sem.at[1],
        recv_sem=zr_sem.at[1],
        device_id=(gx, gy, z_down),
        device_id_type=MESH,
    )
    up_copy.start()
    down_copy.start()

    targets = ((x_in, gy, gz), (x_out, gy, gz), (gx, y_in, gz), (gx, y_out, gz))

    def halo_copy(direction, d):
        flip = 1 if direction < 2 else 2
        if flip == 1:
            q = (xb + 1 + d % 2) % 2 + 2 * ((yb + d // 2) % 2)
        else:
            q = (xb + d % 2) % 2 + 2 * ((yb + 1 + d // 2) % 2)
        rows = pl.ds(2 * q, 2)
        return pltpu.make_async_remote_copy(
            src_ref=vec.at[rows],
            dst_ref=halo.at[direction, rows],
            send_sem=hs_sem.at[direction, d],
            recv_sem=hr_sem.at[direction, d],
            device_id=targets[direction],
            device_id_type=MESH,
        )

    def halo_arrival(direction, d):
        rows = pl.ds(2 * square(d), 2)
        return pltpu.make_async_remote_copy(
            src_ref=vec.at[rows],
            dst_ref=halo.at[direction, rows],
            send_sem=hs_sem.at[direction, d],
            recv_sem=hr_sem.at[direction, d],
            device_id=targets[direction],
            device_id_type=MESH,
        )

    for d in (1, 2, 3, 0):
        for direction in range(4):
            halo_copy(direction, d).start()

    def prepare(z, carry):
        for t in range(t_len):
            blocks[z + 1, t] = right_blocks(vec[z, t])
            vec32[z, t] = vec[z, t].astype(F32)
        return carry

    lax.fori_loop(0, z_len, prepare, 0)

    def prepare_left(q, carry):
        def pieces(dz, t):
            return [vec32[2 * q + dz, t, pl.ds(s, n_vec // 2, stride=2), :] for s in range(2)]

        site = {(dz, t): pieces(dz, t) for dz in range(2) for t in range(2)}
        shape = site[0, 0][0].shape
        lane = lax.broadcasted_iota(jnp.int32, shape, 1)
        low = lane < n_comp

        def pair(one, two):
            real = [jnp.where(low, one[s], rotated(two[s])) for s in range(2)]
            imag = [jnp.where(low, rotated(one[s]), two[s]) for s in range(2)]
            return jnp.concatenate(real + imag, 0).astype(BF16)

        left[q, :, : 2 * n_comp] = pair(site[0, 0], site[0, 1])
        left[q, :, 2 * n_comp :] = pair(site[1, 0], site[1, 1])
        left_t[q, :, : 2 * n_comp] = pair(site[0, 0], site[1, 0])
        left_t[q, :, 2 * n_comp :] = pair(site[0, 1], site[1, 1])
        return carry

    lax.fori_loop(0, q_count, prepare_left, 0)

    up_copy.wait_recv()
    down_copy.wait_recv()
    for t in range(t_len):
        blocks[0, t] = right_blocks(halo_z[0, t])
        blocks[z_len + 1, t] = right_blocks(halo_z[1, t])

    def rs_copy(d, part):
        rows = pl.ds(0, ZT) if part == 0 else pl.ds(ZT, PART - ZT)
        dx, dy = d % 2, d // 2
        return pltpu.make_async_remote_copy(
            src_ref=sendbuf.at[d, rows],
            dst_ref=arrived.at[d, rows],
            send_sem=rs_sem.at[part, d],
            recv_sem=rr_sem.at[part, d],
            device_id=(gx + dx * (1 - 2 * xb), gy + dy * (1 - 2 * yb), gz),
            device_id_type=MESH,
        )

    def local_part(d, put):
        q = square(d)
        z0 = 2 * q
        zero, z_inner, z_outer, t_inner, t_outer = {}, {}, {}, {}, {}
        for dz in range(2):
            z = z0 + dz
            k_in, k_back = (k_zm, k_zp) if dz == 0 else (k_zp, k_zm)
            for t in range(2):
                lhs = jnp.concatenate(
                    [
                        links[z, t, k_zero],
                        links[z0 + 1 - dz, t, k_in],
                        links[z, 1 - t, k_tp],
                        links[z, 1 - t, k_tm],
                    ],
                    0,
                )
                res = hop(lhs, blocks[z + 1, t])
                rows = [res[i * n_comp : (i + 1) * n_comp] for i in range(4)]
                zero[dz, t] = rows[0]
                z_inner[1 - dz, t] = rows[1]
                t_inner[dz, 1 - t] = rows[2] if t == 1 else rows[3]
                t_outer[dz, 1 - t] = rows[3] if t == 1 else rows[2]
                edge = blocks[z0, t] if dz == 0 else blocks[z0 + 3, t]
                z_outer[dz, t] = hop(links[z, t, k_in], edge)
        order = ((0, 0), (0, 1), (1, 0), (1, 1))
        lq = left[q]
        lt = left_t[q]
        total = mm(lq, jnp.concatenate([zero[s] for s in order], 0))
        total = total + mm(lq, jnp.concatenate([z_inner[s] for s in order], 0))
        total = total + mm(lq, jnp.concatenate([t_inner[s] for s in order], 0))
        acc[q] = total
        half = 2 * n_comp
        put(0, fold(mm(lq[:, half:], jnp.concatenate([z_outer[1, 0], z_outer[1, 1]], 0))))
        put(1, fold(mm(lq[:, :half], jnp.concatenate([z_outer[0, 0], z_outer[0, 1]], 0))))
        put(2, fold(mm(lt[:, half:], jnp.concatenate([t_outer[0, 1], t_outer[1, 1]], 0))))
        put(3, fold(mm(lt[:, :half], jnp.concatenate([t_outer[0, 0], t_outer[1, 0]], 0))))

    def halo_part(d, put):
        q = square(d)
        z0 = 2 * q
        lq = left[q]
        sums = []
        for direction in range(4):
            halo_arrival(direction, d).wait_recv()
            rows = []
            for dz in range(2):
                for t in range(2):
                    rows.append(
                        hop(
                            links[z0 + dz, t, k_dirs[direction]],
                            right_blocks(halo[direction, z0 + dz, t]),
                        )
                    )
            sums.append(mm(lq, jnp.concatenate(rows, 0)))
        put(4, fold(acc[q] + sums[0] + sums[2]))
        put(5, fold(sums[1]))
        put(6, fold(sums[3]))

    def put_own(i, value):
        own[i] = value

    def local_step(d, carry):
        def put(i, value):
            sendbuf[d, i] = value.astype(BF16)

        local_part(d, put)
        rs_copy(d, 0).start()
        return carry

    def halo_step(d, carry):
        def put(i, value):
            sendbuf[d, i] = value.astype(BF16)

        halo_part(d, put)
        rs_copy(d, 1).start()
        return carry

    link_copy.wait()
    lax.fori_loop(1, 4, local_step, 0)
    local_part(0, put_own)
    lax.fori_loop(1, 4, halo_step, 0)

    mine = gy // 2 * q_count + square(0)

    def ag_copy(index, device, part):
        rows = pl.ds(0, ZT) if part == 0 else pl.ds(ZT, ALL - ZT)
        return pltpu.make_async_remote_copy(
            src_ref=gathered.at[mine, rows],
            dst_ref=gathered.at[mine, rows],
            send_sem=gs_sem.at[part, index],
            recv_sem=gr_sem.at[part, index],
            device_id=device,
            device_id_type=MESH,
        )

    def put_all(i, value):
        gathered[mine, i] = value.astype(BF16)

    def got(d, i):
        return arrived[d, i].astype(F32)

    for d in range(1, 4):
        rs_copy(d, 0).wait_recv()
    for i in range(ZT):
        put_all(i, own[i] + got(1, i) + got(2, i) + got(3, i))
    for index, (_, _, device) in enumerate(peers):
        ag_copy(index, device, 0).start()

    halo_part(0, put_own)

    for d in range(1, 4):
        rs_copy(d, 1).wait_recv()
    put_all(4, own[4] + got(1, 4) + got(2, 4) + got(3, 4))
    put_all(6 - xb, own[5] + got(2, 5))
    put_all(5 + xb, got(1, 5) + got(3, 5))
    put_all(8 - yb, own[6] + got(1, 6))
    put_all(7 + yb, got(2, 6) + got(3, 6))
    for index, (_, _, device) in enumerate(peers):
        ag_copy(index, device, 1).start()

    kinds = []
    for k in range(ALL):
        kind = jnp.int32(0)
        for i, code in enumerate((9, -9, 27, -27, 0, 1, -1, 3, -3)):
            if i:
                kind = jnp.where(codes[k] == code, i, kind)
        kinds.append(kind)
    capacity = out_ref.shape[3]
    cy_count = n_gy // 2

    up_copy.wait_send()
    down_copy.wait_send()
    for d in range(4):
        for direction in range(4):
            halo_copy(direction, d).wait_send()
    for d in range(1, 4):
        for part in range(2):
            rs_copy(d, part).wait_send()
    for part in range(2):
        for index, (_, _, device) in enumerate(peers):
            ag_copy(index, device, part).wait_recv()

    lines = n_vec // 2

    sources = []
    for slot in range(capacity):
        source = jnp.int32(0)
        for cy in range(cy_count):
            for q in range(q_count):
                here = place_ref[gx // 2, cy, 0, gz * q_count + q]
                source = jnp.where(here == xb * capacity + slot, cy * q_count + q, source)
        sources.append(source)
    for k in range(ALL):
        base = k * capacity * lines
        for slot in range(capacity):
            at = base + slot * lines
            flat[at : at + lines, :] = gathered[sources[slot], kinds[k]].astype(F32)
        for i in range(lines):
            out_ref[0, 0, k, :, 2 * n_comp * i : 2 * n_comp * (i + 1)] = flat[
                pl.ds(base + i, capacity, stride=lines), :
            ]
    for part in range(2):
        for index, (_, _, device) in enumerate(peers):
            ag_copy(index, device, part).wait_send()


def solution(mesh):
    n_gx, n_gy, n_gz = mesh.shape["gx"], mesh.shape["gy"], mesh.shape["gz"]

    def local(links, null_vectors, offsets, place):
        z_len, t_len, stencil, n_comp, width = links.shape[2:]
        n_vec = null_vectors.shape[4]
        q_count = z_len // 2
        aggregates = n_gy // 2 * q_count
        capacity = aggregates // 2
        peers = 2 * n_gy - 1
        lines = n_vec // 2
        dma = pltpu.SemaphoreType.DMA
        result = pl.pallas_call(
            functools.partial(kernel, (n_gx, n_gy, n_gz)),
            out_shape=jax.ShapeDtypeStruct((1, 1, stencil, capacity, 2 * n_vec * n_vec), F32),
            in_specs=[
                pl.BlockSpec(memory_space=pltpu.HBM),
                pl.BlockSpec(memory_space=pltpu.HBM),
                pl.BlockSpec(memory_space=pltpu.SMEM),
                pl.BlockSpec(memory_space=pltpu.SMEM),
            ],
            out_specs=pl.BlockSpec(memory_space=pltpu.VMEM),
            scratch_shapes=[
                pltpu.VMEM((z_len, t_len, stencil, n_comp, width), BF16),
                pltpu.VMEM((z_len, t_len, n_vec, width), BF16),
                pltpu.VMEM((4, z_len, t_len, n_vec, width), BF16),
                pltpu.VMEM((2, t_len, n_vec, width), BF16),
                pltpu.VMEM((z_len + 2, t_len, width, width), BF16),
                pltpu.VMEM((z_len, t_len, n_vec, width), F32),
                pltpu.VMEM((q_count, 2 * n_vec, 4 * n_comp), BF16),
                pltpu.VMEM((q_count, 2 * n_vec, 4 * n_comp), BF16),
                pltpu.VMEM((q_count, 2 * n_vec, width), F32),
                pltpu.VMEM((PART, lines, width), F32),
                pltpu.VMEM((4, PART, lines, width), BF16),
                pltpu.VMEM((4, PART, lines, width), BF16),
                pltpu.VMEM((aggregates, ALL, lines, width), BF16),
                pltpu.VMEM((ALL * capacity * lines, width), F32),
                dma,
                dma,
                dma((4, 4)),
                dma((4, 4)),
                dma((2,)),
                dma((2,)),
                dma((2, 4)),
                dma((2, 4)),
                dma((2, peers)),
                dma((2, peers)),
            ],
            compiler_params=pltpu.CompilerParams(
                collective_id=0, has_side_effects=True, vmem_limit_bytes=63 * 2**20
            ),
            cost_estimate=pl.CostEstimate(
                flops=2 * z_len * t_len * stencil * n_comp * width * 6 * n_vec,
                bytes_accessed=links.size * 2 + null_vectors.size * 2,
                transcendentals=0,
            ),
        )(links, null_vectors, offsets.T, place.swapaxes(2, 3))
        return result.swapaxes(2, 3)

    placed = (
        P("gx", "gy", "gz", None, None, None, None),
        P("gx", "gy", "gz", None, None, None),
        P(),
        P(),
    )
    return jax.shard_map(
        local,
        mesh=mesh,
        in_specs=placed,
        out_specs=P("gx", "gz", None, None, None),
        check_vma=False,
    )
```

time: 93.1 us -> 26.4 us (0.28)
  waiting for transfers between devices: 31.2 us -> 0 us
  Pallas kernels: 0 us -> 24.5 us
  local copies, waits for them, and re-layouts: 18.2 us -> 1.69 us
  blocking collectives: 13.3 us -> 0 us
  other arithmetic: 13.2 us -> 0 us
  starting transfers between devices: 10.3 us -> 0 us
  matrix products: 6.06 us -> 0 us
    ppermute x8 -> x0, waiting for transfers between devices: 31.2 us -> none  [the longest x2 15 us: partner(): return lax.ppermute(value, axis, pairs)]
    pallas_call x0 -> x1, Pallas kernels: none -> 24.5 us  [local(): pl.pallas_call(functools.partial(kernel, (n_gx, n_gy, n_gz)), out_shape=j...]
    all_gather x1 -> x0, blocking collectives: 13.3 us -> none  [local(): incoming = lax.all_gather(sendable[None], 'gy', axis=0, tiled=True)]
    ppermute x8 -> x0, starting transfers between devices: 10.3 us -> none  [the longest x3 4.8 us: with_halo(): lax.ppermute(lax.slice_in_dim(block, block.shape[dim] - width, None, axis...]
    unnamed x31 -> x1, local copies, waits for them, and re-layouts: 7.8 us -> 1.69 us
    dot_general x3 -> x0, matrix products: 6.06 us -> none  [the longest x1 2.55 us: local(): jnp.einsum('ztvq,ztkqu->ztkvu', own_vectors, conj_blocks(hopped), preferr...]
    gather x5 -> x0, local copies, waits for them, and re-layouts: 4.12 us -> none  [the longest x1 2.16 us: local(): neighbour = jnp.take(stacked, chosen, axis=0)]
    add x5 -> x0, other arithmetic: 3.11 us -> none  [the longest x3 2.76 us: local(): (offsets[:, 0] == x_sign).astype(jnp.float32)[None, None, :]]
  transfers between devices with their start and end apart: 8 -> 0, of which waited for: 5 -> 0; matrix products, arithmetic and copies ran while one was open for 23% -> 0% of each run, Pallas kernels for 0% -> 0%
where the time goes in v1:
time: 26.4 us; the launch traced here: 26.2 us
  Pallas kernels  24.5 us (93%)
  local copies, waits for them, and re-layouts  1.69 us (6%)
    pallas_call x1, Pallas kernels, local(): pl.pallas_call(functools.partial(kernel, (n_gx, n_gy, n_gz)), out_shape=j...  24.5 us
    unnamed x1, local copies, waits for them, and re-layouts  1.69 us

profile of v1, /device:TPU:0, one launch (start us, length us, event | category | flops | bytes accessed | tf_op | source)
XLA Modules:
  0.0 26.2 jit_solution(16632258823361035852)
XLA Ops:
  0.0 24.5 %shard_map.46 = f32[1,1,9,4,2048]{4,3,2,1,0:T(4,128)} custom-call(bf16[1,1,8,2,9,64,128]{6,5,4,3,2,1,0:T(8,128)(2,1)} %links_hbm.1, bf16[1,1,8,2,32,128]{5,4,3,2,1,0:T(8,128)(2,1)} %vec_hbm.1, s32[4,9]{1,0:T(4,128)} %bitcast.6, s32[2,2,1,8]{3,2,1,0:T(1,128)} %bitcast.7), custom_call_target="tpu_custom_call" | custom-call | flops 452984832 | bytes 2490368 | tf_op jit(solution)/shard_map/pallas_call | solution.py:410
  24.5 1.7 %copy.7 = f32[1,1,4,9,2048]{4,2,3,1,0:T(4,128)} copy(f32[1,1,4,9,2048]{4,2,3,1,0:T(4,128)} %bitcast.5) | data formatting | bytes 589824

commit v2 on v1

--- a/solution.py
+++ b/solution.py
@@ -126,6 +126,37 @@
     k_dirs = (position(-x_sign), position(x_sign), position(-3 * y_sign), position(3 * y_sign))
 
     vec_copy.wait()
+
+    def prepare(z, carry):
+        for t in range(t_len):
+            blocks[z + 1, t] = right_blocks(vec[z, t])
+            vec32[z, t] = vec[z, t].astype(F32)
+        return carry
+
+    lax.fori_loop(0, z_len, prepare, 0)
+
+    def prepare_left(q, carry):
+        def pieces(dz, t):
+            return [vec32[2 * q + dz, t, pl.ds(s, n_vec // 2, stride=2), :] for s in range(2)]
+
+        site = {(dz, t): pieces(dz, t) for dz in range(2) for t in range(2)}
+        shape = site[0, 0][0].shape
+        lane = lax.broadcasted_iota(jnp.int32, shape, 1)
+        low = lane < n_comp
+
+        def pair(one, two):
+            real = [jnp.where(low, one[s], rotated(two[s])) for s in range(2)]
+            imag = [jnp.where(low, rotated(one[s]), two[s]) for s in range(2)]
+            return jnp.concatenate(real + imag, 0).astype(BF16)
+
+        left[q, :, : 2 * n_comp] = pair(site[0, 0], site[0, 1])
+        left[q, :, 2 * n_comp :] = pair(site[1, 0], site[1, 1])
+        left_t[q, :, : 2 * n_comp] = pair(site[0, 0], site[1, 0])
+        left_t[q, :, 2 * n_comp :] = pair(site[0, 1], site[1, 1])
+        return carry
+
+    lax.fori_loop(0, q_count, prepare_left, 0)
+
     pl.semaphore_wait(barrier, len(peers) + 3)
 
     up_copy = pltpu.make_async_remote_copy(
@@ -179,36 +210,6 @@
     for d in (1, 2, 3, 0):
         for direction in range(4):
             halo_copy(direction, d).start()
-
-    def prepare(z, carry):
-        for t in range(t_len):
-            blocks[z + 1, t] = right_blocks(vec[z, t])
-            vec32[z, t] = vec[z, t].astype(F32)
-        return carry
-
-    lax.fori_loop(0, z_len, prepare, 0)
-
-    def prepare_left(q, carry):
-        def pieces(dz, t):
-            return [vec32[2 * q + dz, t, pl.ds(s, n_vec // 2, stride=2), :] for s in range(2)]
-
-        site = {(dz, t): pieces(dz, t) for dz in range(2) for t in range(2)}
-        shape = site[0, 0][0].shape
-        lane = lax.broadcasted_iota(jnp.int32, shape, 1)
-        low = lane < n_comp
-
-        def pair(one, two):
-            real = [jnp.where(low, one[s], rotated(two[s])) for s in range(2)]
-            imag = [jnp.where(low, rotated(one[s]), two[s]) for s in range(2)]
-            return jnp.concatenate(real + imag, 0).astype(BF16)
-
-        left[q, :, : 2 * n_comp] = pair(site[0, 0], site[0, 1])
-        left[q, :, 2 * n_comp :] = pair(site[1, 0], site[1, 1])
-        left_t[q, :, : 2 * n_comp] = pair(site[0, 0], site[1, 0])
-        left_t[q, :, 2 * n_comp :] = pair(site[0, 1], site[1, 1])
-        return carry
-
-    lax.fori_loop(0, q_count, prepare_left, 0)
 
     up_copy.wait_recv()
     down_copy.wait_recv()
@@ -309,8 +310,6 @@
     link_copy.wait()
     lax.fori_loop(1, 4, local_step, 0)
     local_part(0, put_own)
-    lax.fori_loop(1, 4, halo_step, 0)
-
     mine = gy // 2 * q_count + square(0)
 
     def ag_copy(index, device, part):
@@ -336,6 +335,8 @@
         put_all(i, own[i] + got(1, i) + got(2, i) + got(3, i))
     for index, (_, _, device) in enumerate(peers):
         ag_copy(index, device, 0).start()
+
+    lax.fori_loop(1, 4, halo_step, 0)
 
     halo_part(0, put_own)
 
@@ -389,7 +390,7 @@
         for i in range(lines):
             out_ref[0, 0, k, :, 2 * n_comp * i : 2 * n_comp * (i + 1)] = flat[
                 pl.ds(base + i, capacity, stride=lines), :
-            ]
+            ].astype(BF16)
     for part in range(2):
         for index, (_, _, device) in enumerate(peers):
             ag_copy(index, device, part).wait_send()
@@ -409,7 +410,7 @@
         dma = pltpu.SemaphoreType.DMA
         result = pl.pallas_call(
             functools.partial(kernel, (n_gx, n_gy, n_gz)),
-            out_shape=jax.ShapeDtypeStruct((1, 1, stencil, capacity, 2 * n_vec * n_vec), F32),
+            out_shape=jax.ShapeDtypeStruct((1, 1, stencil, capacity, 2 * n_vec * n_vec), BF16),
             in_specs=[
                 pl.BlockSpec(memory_space=pltpu.HBM),
                 pl.BlockSpec(memory_space=pltpu.HBM),
@@ -452,7 +453,7 @@
                 transcendentals=0,
             ),
         )(links, null_vectors, offsets.T, place.swapaxes(2, 3))
-        return result.swapaxes(2, 3)
+        return result.swapaxes(2, 3).astype(F32)
 
     placed = (
         P("gx", "gy", "gz", None, None, None, None),

time: 26.4 us -> 30.2 us (1.14)
  Pallas kernels: 24.5 us -> 28.4 us
  local copies, waits for them, and re-layouts: 1.69 us -> 0 us
  other arithmetic: 0 us -> 1.65 us
    pallas_call x1, Pallas kernels: 24.5 us -> 28.4 us  [local(): pl.pallas_call(functools.partial(kernel, (n_gx, n_gy, n_gz)), out_shape=j...]
    unnamed x1 -> x0, local copies, waits for them, and re-layouts: 1.69 us -> none
    convert_element_type x0 -> x1, other arithmetic: none -> 1.65 us  [local(): return result.swapaxes(2, 3).astype(F32)]
where the time goes in v2:
time: 30.2 us; the launch traced here: 30.1 us
  Pallas kernels  28.4 us (94%)
  other arithmetic  1.65 us (5%)
    pallas_call x1, Pallas kernels, local(): pl.pallas_call(functools.partial(kernel, (n_gx, n_gy, n_gz)), out_shape=j...  28.4 us
    convert_element_type x1, other arithmetic, local(): return result.swapaxes(2, 3).astype(F32)  1.65 us

profile of v2, /device:TPU:0, one launch (start us, length us, event | category | flops | bytes accessed | tf_op | source)
XLA Modules:
  0.0 30.1 jit_solution(2827848002275363043)
XLA Ops:
  0.0 28.4 %shard_map.46 = bf16[1,1,9,4,2048]{4,3,2,1,0:T(4,128)(2,1)} custom-call(bf16[1,1,8,2,9,64,128]{6,5,4,3,2,1,0:T(8,128)(2,1)} %links_hbm.1, bf16[1,1,8,2,32,128]{5,4,3,2,1,0:T(8,128)(2,1)} %vec_hbm.1, s32[4,9]{1,0:T(4,128)} %bitcast.6, s32[2,2,1,8]{3,2,1,0:T(1,128)} %bitcast.7), custom_call_target="tpu_custom_call" | custom-call | flops 452984832 | bytes 2490368 | tf_op jit(solution)/shard_map/pallas_call | solution.py:411
  28.4 1.6 %convert_bitcast_fusion = f32[1,1,4,9,2048]{4,2,3,1,0:T(4,128)} fusion(bf16[1,1,9,4,2048]{4,3,2,1,0:T(4,128)(2,1)} %shard_map.46), kind=kLoop, calls=%fused_computation | loop fusion | flops 73728 | bytes 442368 | tf_op jit(solution)/shard_map/convert_element_type | solution.py:456

commit v3 on v1

--- a/solution.py
+++ b/solution.py
@@ -177,7 +177,7 @@
         )
 
     for d in (1, 2, 3, 0):
-        for direction in range(4):
+        for direction in (1, 3, 0, 2):
             halo_copy(direction, d).start()
 
     def prepare(z, carry):
@@ -389,7 +389,7 @@
         for i in range(lines):
             out_ref[0, 0, k, :, 2 * n_comp * i : 2 * n_comp * (i + 1)] = flat[
                 pl.ds(base + i, capacity, stride=lines), :
-            ]
+            ].astype(BF16)
     for part in range(2):
         for index, (_, _, device) in enumerate(peers):
             ag_copy(index, device, part).wait_send()
@@ -409,7 +409,7 @@
         dma = pltpu.SemaphoreType.DMA
         result = pl.pallas_call(
             functools.partial(kernel, (n_gx, n_gy, n_gz)),
-            out_shape=jax.ShapeDtypeStruct((1, 1, stencil, capacity, 2 * n_vec * n_vec), F32),
+            out_shape=jax.ShapeDtypeStruct((1, 1, stencil, capacity, 2 * n_vec * n_vec), BF16),
             in_specs=[
                 pl.BlockSpec(memory_space=pltpu.HBM),
                 pl.BlockSpec(memory_space=pltpu.HBM),
@@ -452,7 +452,7 @@
                 transcendentals=0,
             ),
         )(links, null_vectors, offsets.T, place.swapaxes(2, 3))
-        return result.swapaxes(2, 3)
+        return result.swapaxes(2, 3).astype(F32)
 
     placed = (
         P("gx", "gy", "gz", None, None, None, None),

time: 26.4 us -> 25.7 us (0.973)
  local copies, waits for them, and re-layouts: 1.69 us -> 0 us
  other arithmetic: 0 us -> 1.65 us
  Pallas kernels: 24.5 us -> 23.9 us
    unnamed x1 -> x0, local copies, waits for them, and re-layouts: 1.69 us -> none
    convert_element_type x0 -> x1, other arithmetic: none -> 1.65 us  [local(): return result.swapaxes(2, 3).astype(F32)]
    pallas_call x1, Pallas kernels: 24.5 us -> 23.9 us  [local(): pl.pallas_call(functools.partial(kernel, (n_gx, n_gy, n_gz)), out_shape=j...]
where the time goes in v3:
time: 25.7 us; the launch traced here: 25.6 us
  Pallas kernels  23.9 us (93%)
  other arithmetic  1.65 us (6%)
    pallas_call x1, Pallas kernels, local(): pl.pallas_call(functools.partial(kernel, (n_gx, n_gy, n_gz)), out_shape=j...  23.9 us
    convert_element_type x1, other arithmetic, local(): return result.swapaxes(2, 3).astype(F32)  1.65 us

profile of v3, /device:TPU:0, one launch (start us, length us, event | category | flops | bytes accessed | tf_op | source)
XLA Modules:
  0.0 25.6 jit_solution(2725378764149891204)
XLA Ops:
  0.0 23.9 %shard_map.46 = bf16[1,1,9,4,2048]{4,3,2,1,0:T(4,128)(2,1)} custom-call(bf16[1,1,8,2,9,64,128]{6,5,4,3,2,1,0:T(8,128)(2,1)} %links_hbm.1, bf16[1,1,8,2,32,128]{5,4,3,2,1,0:T(8,128)(2,1)} %vec_hbm.1, s32[4,9]{1,0:T(4,128)} %bitcast.6, s32[2,2,1,8]{3,2,1,0:T(1,128)} %bitcast.7), custom_call_target="tpu_custom_call" | custom-call | flops 452984832 | bytes 2490368 | tf_op jit(solution)/shard_map/pallas_call | solution.py:410
  23.9 1.6 %convert_bitcast_fusion = f32[1,1,4,9,2048]{4,2,3,1,0:T(4,128)} fusion(bf16[1,1,9,4,2048]{4,3,2,1,0:T(4,128)(2,1)} %shard_map.46), kind=kLoop, calls=%fused_computation | loop fusion | flops 73728 | bytes 442368 | tf_op jit(solution)/shard_map/convert_element_type | solution.py:455

commit v4 on v3

--- a/solution.py
+++ b/solution.py
@@ -94,6 +94,8 @@
             if dx or dy:
                 peers.append((dx, dy, (gx + dx * (1 - 2 * xb), (gy + dy) % n_gy, gz)))
 
+    peers.sort(key=lambda peer: -(peer[0] + min(peer[1], n_gy - peer[1])))
+
     barrier = pltpu.get_barrier_semaphore()
     for _, _, device in peers:
         pl.semaphore_signal(barrier, inc=1, device_id=device, device_id_type=MESH)
@@ -176,7 +178,7 @@
             device_id_type=MESH,
         )
 
-    for d in (1, 2, 3, 0):
+    for d in (3, 2, 1, 0):
         for direction in (1, 3, 0, 2):
             halo_copy(direction, d).start()
 
@@ -290,7 +292,9 @@
     def put_own(i, value):
         own[i] = value
 
-    def local_step(d, carry):
+    def local_step(step, carry):
+        d = 4 - step
+
         def put(i, value):
             sendbuf[d, i] = value.astype(BF16)
 
@@ -298,7 +302,9 @@
         rs_copy(d, 0).start()
         return carry
 
-    def halo_step(d, carry):
+    def halo_step(step, carry):
+        d = 4 - step
+
         def put(i, value):
             sendbuf[d, i] = value.astype(BF16)
 

time: 25.7 us -> 25.5 us (level)
  no operation moved by 1% of the time
where the time goes in v4:
time: 25.5 us; the launch traced here: 25.3 us
  Pallas kernels  23.7 us (93%)
  other arithmetic  1.65 us (6%)
    pallas_call x1, Pallas kernels, local(): pl.pallas_call(functools.partial(kernel, (n_gx, n_gy, n_gz)), out_shape=j...  23.7 us
    convert_element_type x1, other arithmetic, local(): return result.swapaxes(2, 3).astype(F32)  1.65 us

profile of v4, /device:TPU:0, one launch (start us, length us, event | category | flops | bytes accessed | tf_op | source)
XLA Modules:
  0.0 25.3 jit_solution(9491137265235887383)
XLA Ops:
  0.0 23.7 %shard_map.46 = bf16[1,1,9,4,2048]{4,3,2,1,0:T(4,128)(2,1)} custom-call(bf16[1,1,8,2,9,64,128]{6,5,4,3,2,1,0:T(8,128)(2,1)} %links_hbm.1, bf16[1,1,8,2,32,128]{5,4,3,2,1,0:T(8,128)(2,1)} %vec_hbm.1, s32[4,9]{1,0:T(4,128)} %bitcast.6, s32[2,2,1,8]{3,2,1,0:T(1,128)} %bitcast.7), custom_call_target="tpu_custom_call" | custom-call | flops 452984832 | bytes 2490368 | tf_op jit(solution)/shard_map/pallas_call | solution.py:416
  23.7 1.6 %convert_bitcast_fusion = f32[1,1,4,9,2048]{4,2,3,1,0:T(4,128)} fusion(bf16[1,1,9,4,2048]{4,3,2,1,0:T(4,128)(2,1)} %shard_map.46), kind=kLoop, calls=%fused_computation | loop fusion | flops 73728 | bytes 442368 | tf_op jit(solution)/shard_map/convert_element_type | solution.py:461
